TPU v7x, 512 devices: a whole 4x4x16 slice. The times are simulated.
512 devices in a mesh: region: 64 (over z, x), member: 8 (over y, core).
Axes of the slice: x: 4, y: 4, z: 16, core: 2. Of those that a mesh axis runs over, the one named last changes fastest.
Arguments:
- perturbations: bfloat16 [80, 2, 64, 8192], P('member', None, None, 'region'), may hold values from -0.65625 to 0.65625
- control: float32 [80, 64, 8192], P('member', None, 'region'), may hold values from -6 to 6
- vertical_loc: bfloat16 [64, 64], replicated, may hold values from -0.75 to 0.75
- block_kernels: bfloat16 [4, 128, 128], replicated, may hold values from -0.3125 to 0.3125
- loc_pattern: int32 [64, 3], replicated, may hold values from 0 to 3
- obs_region: int32 [65536, 1], P('region'), may hold values from 0 to 63; in each aligned block of 128 rows (0 to 127, 128 to 255, ...) at most 4 rows name the same one
- obs_slot: int32 [65536], P('region'), may hold values from 0 to 1
- obs_cell: int32 [65536], P('region'), may hold values from 0 to 127
- innovations: float32 [64, 65536], P(None, 'region'), may hold values from -12 to 12
- obs_weight: float32 [512, 128, 128], P('region'), may hold values from -0.0375 to 2, as said below
Outputs:
- analysis: float32 [80, 64, 8192], P('member', None, 'region')
Inputs may be any that keep to these rules, and one draw needn't show every extreme that they name: `obs_region`: in each aligned block of 128 rows, no region is named by more than 4 rows. `obs_weight`: each tile is symmetric, and in each row the diagonal entry exceeds the sum of the magnitudes of the other entries.
All inputs are finite; a program needn't handle non-finite values.
Results may differ from a plain program's by a relative error of at most 0.013.
Values may be sent and summed in bfloat16 or wider, within the bound.
A program may use at most 64 MiB of HBM per device.

v0:
```python
import jax
import jax.numpy as jnp
from jax import lax
from jax.sharding import PartitionSpec as P

SLOTS = 2
BLOCK = 128
TILE = 128
ITERS = 2
CELLS_DEV = 128
OBS_DEV = 1024


def padded_2(block, sides, width):
    for axis, dim in sides:
        count = lax.axis_size(axis)
        forward = [(i, i + 1) for i in range(count - 1)]
        backward = [(target, source) for source, target in forward]
        low = lax.ppermute(
            lax.slice_in_dim(block, block.shape[dim] - width, None, axis=dim), axis, forward
        )
        high = lax.ppermute(lax.slice_in_dim(block, 0, width, axis=dim), axis, backward)
        block = jnp.concatenate([low, block, high], axis=dim)
    return block


def pick_kernels(block_kernels, indices):
    kernel_ids = jnp.arange(block_kernels.shape[0], dtype=jnp.int32)
    onehot = (indices[:, None] == kernel_ids[None, :]).astype(jnp.bfloat16)
    return jnp.einsum(
        "bk,kij->bij", onehot, block_kernels, preferred_element_type=jnp.float32
    ).astype(jnp.bfloat16)


def spread_blocks(values, kernel_list, transposed):
    padded = padded_2(values, (("region", 2),), BLOCK)
    member_count, level_count, cell_count = values.shape
    block_count = cell_count // BLOCK
    summed = jnp.zeros((member_count, level_count, block_count, BLOCK), jnp.float32)
    for offset in range(3):
        first_cell = (2 - offset) * BLOCK if transposed else offset * BLOCK
        window = padded[:, :, first_cell : first_cell + cell_count].reshape(
            member_count, level_count, block_count, BLOCK
        )
        if transposed:
            summed = summed + jnp.einsum(
                "mlbj,bkj->mlbk", window, kernel_list[offset], preferred_element_type=jnp.float32
            )
        else:
            summed = summed + jnp.einsum(
                "mlbk,bkj->mlbj", window, kernel_list[offset], preferred_element_type=jnp.float32
            )
    return summed.reshape(member_count, level_count, cell_count)


def route_rows(targets, sub_count, regions, capacity):
    obs_total = targets.shape[0]
    per_sub = obs_total // sub_count
    grouped = targets.reshape(sub_count, per_sub)
    region_ids = jnp.arange(regions, dtype=jnp.int32)
    onehot = (grouped[:, :, None] == region_ids[None, None, :]).astype(jnp.int32)
    before = jnp.cumsum(onehot, axis=1) - onehot
    ranking = jnp.sum(before * onehot, axis=2)
    sub_index = jnp.arange(sub_count, dtype=jnp.int32)[:, None]
    position = (grouped * (sub_count * capacity) + sub_index * capacity + ranking).reshape(
        obs_total
    )
    slot_row = jnp.full((regions * sub_count * capacity,), obs_total, jnp.int32)
    slot_row = slot_row.at[position].set(jnp.arange(obs_total, dtype=jnp.int32))
    return (position, slot_row)


def squared_norm(vector):
    return lax.psum(jnp.sum(vector * vector), ("region", "member"))


def local(
    perturbations,
    control,
    vertical_loc,
    block_kernels,
    loc_pattern,
    obs_region,
    obs_slot,
    obs_cell,
    innovations,
    obs_weight,
):
    regions = lax.axis_size("region")
    members = lax.axis_size("member")
    region_index = lax.axis_index("region")
    member_index = lax.axis_index("member")
    nblocks = CELLS_DEV // BLOCK
    capacity = max(2, 2 * (OBS_DEV // members) // regions)
    group_rows = OBS_DEV // members
    pattern_pad = jnp.pad(loc_pattern, ((1, 1), (0, 0)))
    pattern_rows = lax.dynamic_slice_in_dim(pattern_pad, region_index * nblocks, nblocks + 2, 0)
    forward_list = [
        pick_kernels(block_kernels, pattern_rows[1 : nblocks + 1, offset]) for offset in range(3)
    ]
    backward_list = [
        pick_kernels(block_kernels, pattern_rows[2 - offset : 2 - offset + nblocks, offset])
        for offset in range(3)
    ]
    cell_codes = obs_slot * CELLS_DEV + obs_cell
    targets = obs_region[:, 0]
    sub_count = 1
    first_row = member_index * group_rows
    targets = lax.dynamic_slice_in_dim(targets, first_row, group_rows, 0)
    obs_codes = lax.dynamic_slice_in_dim(cell_codes, first_row, group_rows, 0)
    innovation_rows = lax.dynamic_slice_in_dim(innovations, first_row, group_rows, 1)
    weight_tiles = lax.dynamic_slice_in_dim(
        obs_weight, member_index * (group_rows // TILE), group_rows // TILE, 0
    )
    position, slot_row = route_rows(targets, sub_count, regions, capacity)
    padded_codes = jnp.concatenate([obs_codes, jnp.full((1,), SLOTS * CELLS_DEV, jnp.int32)])
    region_codes = lax.all_to_all(
        padded_codes[slot_row], "region", split_axis=0, concat_axis=0, tiled=True
    )

    def apply_operator(vector, with_innovation):
        spread = spread_blocks(vector.astype(jnp.bfloat16), forward_list, False).astype(
            jnp.bfloat16
        )
        weights = jnp.einsum(
            "lk,mkc->mlc", vertical_loc, spread, preferred_element_type=jnp.float32
        )
        member_sum = jnp.sum(perturbations.astype(jnp.float32) * weights[:, None], axis=0)
        increment = lax.psum(member_sum.astype(jnp.bfloat16), "member").astype(jnp.float32)
        levels_here = increment.shape[1]
        flattened = increment.transpose(1, 0, 2).reshape(levels_here, SLOTS * CELLS_DEV)
        flat_padded = jnp.concatenate([flattened, jnp.zeros((levels_here, 1), jnp.float32)], axis=1)
        sampled = jnp.take(flat_padded, region_codes, axis=1)
        at_holders = lax.all_to_all(
            sampled.astype(jnp.bfloat16), "region", split_axis=1, concat_axis=1, tiled=True
        ).astype(sampled.dtype)
        departures = jnp.take(at_holders, position, axis=1)
        if with_innovation:
            departures = departures - innovation_rows
        obs_count = departures.shape[1]
        weighted = jnp.einsum(
            "ltk,tkj->ltj",
            departures.reshape(levels_here, obs_count // TILE, TILE),
            weight_tiles,
            precision=lax.Precision.HIGHEST,
        ).reshape(levels_here, obs_count)
        weighted_pad = jnp.concatenate([weighted, jnp.zeros((levels_here, 1), jnp.float32)], axis=1)
        returned = jnp.take(weighted_pad, slot_row, axis=1)
        at_regions = lax.all_to_all(
            returned.astype(jnp.bfloat16), "region", split_axis=1, concat_axis=1, tiled=True
        ).astype(returned.dtype)
        adjoint_flat = (
            jnp.zeros((levels_here, SLOTS * CELLS_DEV + 1), jnp.float32)
            .at[:, region_codes]
            .add(at_regions)
        )
        adjoint_part = (
            adjoint_flat[:, : SLOTS * CELLS_DEV]
            .reshape(levels_here, SLOTS, CELLS_DEV)
            .transpose(1, 0, 2)
        )
        adjoint_field = lax.psum(adjoint_part.astype(jnp.bfloat16), "member").astype(jnp.float32)
        projected = jnp.sum(perturbations.astype(jnp.float32) * adjoint_field[None], axis=1).astype(
            jnp.bfloat16
        )
        lifted = jnp.einsum(
            "kl,mkc->mlc", vertical_loc, projected, preferred_element_type=jnp.float32
        ).astype(jnp.bfloat16)
        return vector + spread_blocks(lifted, backward_list, True)

    solution = control
    residual = -apply_operator(control, True)
    direction = residual
    norm_now = squared_norm(residual)
    for iteration in range(ITERS):
        curved = apply_operator(direction, False)
        step_size = norm_now / lax.psum(jnp.sum(direction * curved), ("region", "member"))
        solution = solution + step_size * direction
        if iteration + 1 < ITERS:
            residual = residual - step_size * curved
            norm_next = squared_norm(residual)
            direction = residual + norm_next / norm_now * direction
            norm_now = norm_next
    return solution


def solution(mesh):
    placed = (
        P("member", None, None, "region"),
        P("member", None, "region"),
        P(),
        P(),
        P(),
        P("region", None),
        P("region"),
        P("region"),
        P(None, "region"),
        P("region", None, None),
    )
    return jax.shard_map(
        local, mesh=mesh, in_specs=placed, out_specs=P("member", None, "region"), check_vma=False
    )
```

profile of v0, /device:TPU:1, one launch (start us, length us, event | category | flops | bytes accessed | tf_op | source)
XLA Modules:
  0.0 705.3 jit_solution(5784242501238272621)
XLA Ops:
  2.4 4.6 collective-permute-start
  12.6 20.4 %all-to-all-start = ((s32[64,4,1]{1,2,0:T(1,128)}), s32[64,4,1]{1,2,0:T(1,128)S(1)}, u32[]{:S(2)}, u32[]{:S(2)}) async-start(s32[64,4,1]{1,2,0:T(1,128)} %bitcast.8), calls=%async_computation | async-start | bytes 65536 | tf_op jit(solution)/shard_map/all_to_all | solution.py:117
  39.4 6.9 all-to-all-done
  48.4 23.6 %psum.70 = bf16[64,256]{0,1:T(8,128)(2,1)S(1)} all-reduce(bf16[64,256]{0,1:T(8,128)(2,1)S(1)} %bitcast.318), channel_id=1, replica_groups=mesh['region'=64,'member'=8] {'member'}, use_global_device_ids=true, to_apply=%region_4.5 | all-reduce | flops 16384 | bytes 65536 | tf_op jit(solution)/shard_map/psum | solution.py:129
  73.7 7.5 %all-to-all-start.1 = ((bf16[64,2,128]{2,1,0:T(2,128)(2,1)}), bf16[64,2,128]{2,1,0:T(2,128)(2,1)S(1)}, u32[]{:S(2)}, u32[]{:S(2)}) async-start(bf16[64,2,128]{2,1,0:T(2,128)(2,1)} %reshape.599), calls=%async_computation.1 | async-start | bytes 65536 | tf_op jit(solution)/shard_map/all_to_all | solution.py:134
  83.6 11.0 %all-to-all-done.1 = bf16[64,2,128]{2,1,0:T(2,128)(2,1)S(1)} async-done(((bf16[64,2,128]{2,1,0:T(2,128)(2,1)}), bf16[64,2,128]{2,1,0:T(2,128)(2,1)S(1)}, u32[]{:S(2)}, u32[]{:S(2)}) %all-to-all-start.1) | async-done | bytes 32800 | tf_op jit(solution)/shard_map/all_to_all | solution.py:134
  97.5 4.6 all-to-all-start.2
  102.1 13.5 %all-to-all-done.2 = bf16[64,2,128]{2,1,0:T(2,128)(2,1)S(1)} async-done(((bf16[64,2,128]{2,1,0:T(2,128)(2,1)}), bf16[64,2,128]{2,1,0:T(2,128)(2,1)S(1)}, u32[]{:S(2)}, u32[]{:S(2)}) %all-to-all-start.2) | async-done | bytes 32800 | tf_op jit(solution)/shard_map/all_to_all | solution.py:149
  117.3 26.1 %psum.71 = bf16[2,64,128]{2,1,0:T(8,128)(2,1)S(1)} all-reduce(bf16[2,64,128]{2,1,0:T(8,128)(2,1)S(1)} %bitcast.328), channel_id=1, replica_groups=mesh['region'=64,'member'=8] {'member'}, use_global_device_ids=true, to_apply=%region_6.10 | all-reduce | flops 16384 | bytes 65536 | tf_op jit(solution)/shard_map/psum | solution.py:162
  148.8 3.6 collective-permute-done.2
  154.0 4.0 collective-permute-start.4
  160.8 26.9 %psum.73 = bf16[64,256]{0,1:T(8,128)(2,1)S(1)} all-reduce(bf16[64,256]{0,1:T(8,128)(2,1)S(1)} %bitcast.322), channel_id=1, replica_groups=mesh['region'=64,'member'=8] {'member'}, use_global_device_ids=true, to_apply=%region_11.15 | all-reduce | flops 16384 | bytes 65536 | tf_op jit(solution)/shard_map/psum | solution.py:129
  188.7 27.8 %all_to_all.69 = bf16[64,2,128]{2,1,0:T(2,128)(2,1)S(1)} all-to-all(bf16[64,2,128]{2,1,0:T(2,128)(2,1)S(1)} %reshape.603), channel_id=1, replica_groups=mesh['region'=64,'member'=8] {'region'}, dimensions={0} | all-to-all | bytes 65536 | tf_op jit(solution)/shard_map/all_to_all | solution.py:134
  218.9 17.4 %all_to_all.70 = bf16[64,2,128]{2,1,0:T(2,128)(2,1)S(1)} all-to-all(bf16[64,2,128]{2,1,0:T(2,128)(2,1)S(1)} %reshape.605), channel_id=1, replica_groups=mesh['region'=64,'member'=8] {'region'}, dimensions={0} | all-to-all | bytes 65536 | tf_op jit(solution)/shard_map/all_to_all | solution.py:149
  238.0 25.9 %psum.74 = bf16[2,64,128]{2,1,0:T(8,128)(2,1)S(1)} all-reduce(bf16[2,64,128]{2,1,0:T(8,128)(2,1)S(1)} %bitcast.329), channel_id=1, replica_groups=mesh['region'=64,'member'=8] {'member'}, use_global_device_ids=true, to_apply=%region_13.17 | all-reduce | flops 16384 | bytes 65536 | tf_op jit(solution)/shard_map/psum | solution.py:162
  273.8 105.6 %all-reduce.7 = (f32[]{:T(128)}, f32[]{:T(128)}) all-reduce(f32[]{:T(128)} %get-tuple-element.8, f32[]{:T(128)} %get-tuple-element.6), channel_id=1, replica_groups=mesh['region'=64,'member'=8] {'region','member'}, use_global_device_ids=true, to_apply=%region_9.13 | all-reduce | flops 2 | bytes 16 | tf_op jit(solution)/shard_map/psum | solution.py:74
  381.3 99.4 %psum.76 = f32[]{:T(128)} all-reduce(f32[]{:T(128)} %multiply_reduce_fusion), channel_id=1, replica_groups=mesh['region'=64,'member'=8] {'region','member'}, use_global_device_ids=true, to_apply=%region_18.22 | all-reduce | flops 1 | bytes 8 | tf_op jit(solution)/shard_map/psum | solution.py:74
  483.4 4.0 collective-permute-start.8
  490.5 22.6 %psum.77 = bf16[64,256]{0,1:T(8,128)(2,1)S(1)} all-reduce(bf16[64,256]{0,1:T(8,128)(2,1)S(1)} %bitcast.326), channel_id=1, replica_groups=mesh['region'=64,'member'=8] {'member'}, use_global_device_ids=true, to_apply=%region_20.24 | all-reduce | flops 16384 | bytes 65536 | tf_op jit(solution)/shard_map/psum | solution.py:129
  514.2 26.2 %all_to_all.71 = bf16[64,2,128]{2,1,0:T(2,128)(2,1)S(1)} all-to-all(bf16[64,2,128]{2,1,0:T(2,128)(2,1)S(1)} %reshape.607), channel_id=1, replica_groups=mesh['region'=64,'member'=8] {'region'}, dimensions={0} | all-to-all | bytes 65536 | tf_op jit(solution)/shard_map/all_to_all | solution.py:134
  542.8 17.4 %all_to_all.72 = bf16[64,2,128]{2,1,0:T(2,128)(2,1)S(1)} all-to-all(bf16[64,2,128]{2,1,0:T(2,128)(2,1)S(1)} %reshape.609), channel_id=1, replica_groups=mesh['region'=64,'member'=8] {'region'}, dimensions={0} | all-to-all | bytes 65536 | tf_op jit(solution)/shard_map/all_to_all | solution.py:149
  561.8 25.9 %psum.78 = bf16[2,64,128]{2,1,0:T(8,128)(2,1)S(1)} all-reduce(bf16[2,64,128]{2,1,0:T(8,128)(2,1)S(1)} %bitcast.330), channel_id=1, replica_groups=mesh['region'=64,'member'=8] {'member'}, use_global_device_ids=true, to_apply=%region_22.26 | all-reduce | flops 16384 | bytes 65536 | tf_op jit(solution)/shard_map/psum | solution.py:162
  593.1 3.6 collective-permute-done.10
  597.7 105.5 %psum.79 = f32[]{:T(128)} all-reduce(f32[]{:T(128)} %fusion.28), channel_id=1, replica_groups=mesh['region'=64,'member'=8] {'region','member'}, use_global_device_ids=true, to_apply=%region_25.29 | all-reduce | flops 1 | bytes 8 | tf_op jit(solution)/shard_map/psum | solution.py:177
  (158 shorter events, 66.7 us)
Async XLA Ops:
  0.0 95.3 %copy-start = (f32[8,128,128]{2,1,0:T(8,128)S(1)}, f32[8,128,128]{2,1,0:T(8,128)}, u32[]{:S(2)}) copy-start(f32[8,128,128]{2,1,0:T(8,128)} %param.25) | copy-start | bytes 1572868
  1.1 45.4 %collective-permute-start.1 = (bf16[10,64,128]{2,1,0:T(8,128)(2,1)S(1)}, bf16[10,64,128]{2,1,0:T(8,128)(2,1)S(1)}, u32[]{:S(2)}, u32[]{:S(2)}) collective-permute-start(bf16[10,64,128]{2,1,0:T(8,128)(2,1)S(1)} %convert_element_type.222), channel_id=1, source_target_pairs={{8,0},{16,8},{24,16},{32,24},{40,32},{48,40},{56,48},{64,56},{72,6... | collective-permute-start | bytes 491528 | tf_op jit(solution)/shard_map/ppermute | solution.py:22
  2.4 44.3 %collective-permute-start = (bf16[10,64,128]{2,1,0:T(8,128)(2,1)S(1)}, bf16[10,64,128]{2,1,0:T(8,128)(2,1)S(1)}, u32[]{:S(2)}, u32[]{:S(2)}) collective-permute-start(bf16[10,64,128]{2,1,0:T(8,128)(2,1)S(1)} %convert_element_type.222), channel_id=1, source_target_pairs={{0,8},{8,16},{16,24},{24,32},{32,40},{40,48},{48,56},{56,64},{64,7... | collective-permute-start | bytes 491528 | tf_op jit(solution)/shard_map/ppermute | solution.py:19
  7.0 0.7 copy-start.5
  7.0 0.7 copy-start.4
  9.9 25.2 %copy-start.7 = (bf16[4,128,128]{2,1,0:T(8,128)(2,1)S(1)}, bf16[4,128,128]{2,1,0:T(8,128)(2,1)}, u32[]{:S(2)}) copy-start(bf16[4,128,128]{2,1,0:T(8,128)(2,1)} %param.19) | copy-start | bytes 393220
  12.6 33.7 %all-to-all-start = ((s32[64,4,1]{1,2,0:T(1,128)}), s32[64,4,1]{1,2,0:T(1,128)S(1)}, u32[]{:S(2)}, u32[]{:S(2)}) async-start(s32[64,4,1]{1,2,0:T(1,128)} %bitcast.8), calls=%async_computation | async-start | bytes 65536 | tf_op jit(solution)/shard_map/all_to_all | solution.py:117
  33.6 0.7 copy-start.6
  46.5 0.7 copy-start.3
  47.2 1.0 copy-start.1
  73.7 20.9 %all-to-all-start.1 = ((bf16[64,2,128]{2,1,0:T(2,128)(2,1)}), bf16[64,2,128]{2,1,0:T(2,128)(2,1)S(1)}, u32[]{:S(2)}, u32[]{:S(2)}) async-start(bf16[64,2,128]{2,1,0:T(2,128)(2,1)} %reshape.599), calls=%async_computation.1 | async-start | bytes 65536 | tf_op jit(solution)/shard_map/all_to_all | solution.py:134
  97.5 18.1 %all-to-all-start.2 = ((bf16[64,2,128]{2,1,0:T(2,128)(2,1)}), bf16[64,2,128]{2,1,0:T(2,128)(2,1)S(1)}, u32[]{:S(2)}, u32[]{:S(2)}) async-start(bf16[64,2,128]{2,1,0:T(2,128)(2,1)} %reshape.601), calls=%async_computation.2 | async-start | bytes 65536 | tf_op jit(solution)/shard_map/all_to_all | solution.py:149
  143.8 4.8 collective-permute-start.3
  146.4 6.1 collective-permute-start.2
  147.9 4.6 copy-start.2
  152.7 6.1 collective-permute-start.5
  154.0 6.2 collective-permute-start.4
  264.2 4.8 collective-permute-start.7
  266.8 6.1 collective-permute-start.6
  482.1 7.0 collective-permute-start.9
  483.4 6.5 collective-permute-start.8
  588.0 4.8 collective-permute-start.11
  590.7 6.1 collective-permute-start.10
where the time goes:
time: 707 us; the launch traced here: 705 us
  blocking collectives  550 us (78%)
  starting transfers between devices  60.6 us (9%)
  waiting for transfers between devices  48.5 us (7%)
  local copies, waits for them, and re-layouts  19.2 us (3%)
  matrix products  11.3 us (2%)
  other arithmetic  10.8 us (2%)
    psum x2, blocking collectives, squared_norm(): return lax.psum(jnp.sum(vector * vector), ('region', 'member'))  205 us
    psum x1, blocking collectives, local(): lax.psum(jnp.sum(direction * curved), ('region', 'member'))  105 us
    psum x3, blocking collectives, apply_operator(): lax.psum(adjoint_part.astype(jnp.bfloat16), 'member').astype(jnp.float32)  77.9 us
    psum x3, blocking collectives, apply_operator(): lax.psum(member_sum.astype(jnp.bfloat16), 'member').astype(jnp.float32)  73.1 us
    all_to_all x2, blocking collectives, apply_operator(): lax.all_to_all(sampled.astype(jnp.bfloat16), 'region', split_axis=1, conc...  54.1 us
    all_to_all x2, blocking collectives, apply_operator(): lax.all_to_all(returned.astype(jnp.bfloat16), 'region', split_axis=1, con...  34.7 us
    all_to_all x1, starting transfers between devices, local(): lax.all_to_all(padded_codes[slot_row], 'region', split_axis=0, concat_axi...  20.4 us
    ppermute x6, starting transfers between devices, padded_2(): lax.ppermute(lax.slice_in_dim(block, block.shape[dim] - width, None, axis...  20.3 us
  transfers between devices with their start and end apart: 15, of which 13 were waited for; matrix products, arithmetic and copies ran while one was open for 2% of the time, Pallas kernels for 0%

commit v1 on v0

--- a/solution.py
+++ b/solution.py
@@ -159,7 +159,9 @@
             .reshape(levels_here, SLOTS, CELLS_DEV)
             .transpose(1, 0, 2)
         )
-        adjoint_field = lax.psum(adjoint_part.astype(jnp.bfloat16), "member").astype(jnp.float32)
+        adjoint_field = jnp.sum(
+            lax.all_gather(adjoint_part.astype(jnp.bfloat16), "member"), axis=0
+        ).astype(jnp.float32)
         projected = jnp.sum(perturbations.astype(jnp.float32) * adjoint_field[None], axis=1).astype(
             jnp.bfloat16
         )

time: 707 us -> 678 us (0.959)
  blocking collectives: 550 us -> 518 us
    psum x3 -> x0, blocking collectives: 77.9 us -> none  [apply_operator(): lax.psum(adjoint_part.astype(jnp.bfloat16), 'member').astype(jnp.float32)]
    all_gather x0 -> x3, blocking collectives: none -> 55.7 us  [apply_operator(): lax.all_gather(adjoint_part.astype(jnp.bfloat16), 'member')]
where the time goes in v1:
time: 678 us; the launch traced here: 677 us
  blocking collectives  518 us (76%)
  starting transfers between devices  60.4 us (9%)
  waiting for transfers between devices  52 us (8%)
  local copies, waits for them, and re-layouts  19.2 us (3%)
  matrix products  11.3 us (2%)
  other arithmetic  10.9 us (2%)
    psum x2, blocking collectives, squared_norm(): return lax.psum(jnp.sum(vector * vector), ('region', 'member'))  202 us
    psum x1, blocking collectives, local(): lax.psum(jnp.sum(direction * curved), ('region', 'member'))  102 us
    psum x3, blocking collectives, apply_operator(): lax.psum(member_sum.astype(jnp.bfloat16), 'member').astype(jnp.float32)  69.5 us
    all_gather x3, blocking collectives, apply_operator(): lax.all_gather(adjoint_part.astype(jnp.bfloat16), 'member')  55.7 us
    all_to_all x2, blocking collectives, apply_operator(): lax.all_to_all(sampled.astype(jnp.bfloat16), 'region', split_axis=1, conc...  54.6 us
    all_to_all x2, blocking collectives, apply_operator(): lax.all_to_all(returned.astype(jnp.bfloat16), 'region', split_axis=1, con...  34.7 us
    all_to_all x1, starting transfers between devices, local(): lax.all_to_all(padded_codes[slot_row], 'region', split_axis=0, concat_axi...  20.4 us
    ppermute x6, starting transfers between devices, padded_2(): lax.ppermute(lax.slice_in_dim(block, block.shape[dim] - width, None, axis...  20.2 us
  transfers between devices with their start and end apart: 15, of which 13 were waited for; matrix products, arithmetic and copies ran while one was open for 2% of the time, Pallas kernels for 0%

profile of v1, /device:TPU:1, one launch (start us, length us, event | category | flops | bytes accessed | tf_op | source)
XLA Modules:
  0.0 676.8 jit_solution(7527511993768962413)
XLA Ops:
  2.4 4.6 collective-permute-start
  12.6 20.4 %all-to-all-start = ((s32[64,4,1]{1,2,0:T(1,128)}), s32[64,4,1]{1,2,0:T(1,128)S(1)}, u32[]{:S(2)}, u32[]{:S(2)}) async-start(s32[64,4,1]{1,2,0:T(1,128)} %bitcast.8), calls=%async_computation | async-start | bytes 65536 | tf_op jit(solution)/shard_map/all_to_all | solution.py:117
  39.4 6.9 %all-to-all-done = s32[64,4,1]{1,2,0:T(1,128)S(1)} async-done(((s32[64,4,1]{1,2,0:T(1,128)}), s32[64,4,1]{1,2,0:T(1,128)S(1)}, u32[]{:S(2)}, u32[]{:S(2)}) %all-to-all-start) | async-done | bytes 1056 | tf_op jit(solution)/shard_map/all_to_all | solution.py:117
  48.4 23.6 %psum.49 = bf16[64,256]{0,1:T(8,128)(2,1)S(1)} all-reduce(bf16[64,256]{0,1:T(8,128)(2,1)S(1)} %bitcast.324), channel_id=1, replica_groups=mesh['region'=64,'member'=8] {'member'}, use_global_device_ids=true, to_apply=%region_4.5 | all-reduce | flops 16384 | bytes 65536 | tf_op jit(solution)/shard_map/psum | solution.py:129
  73.7 7.5 %all-to-all-start.1 = ((bf16[64,2,128]{2,1,0:T(2,128)(2,1)}), bf16[64,2,128]{2,1,0:T(2,128)(2,1)S(1)}, u32[]{:S(2)}, u32[]{:S(2)}) async-start(bf16[64,2,128]{2,1,0:T(2,128)(2,1)} %reshape.608), calls=%async_computation.1 | async-start | bytes 65536 | tf_op jit(solution)/shard_map/all_to_all | solution.py:134
  83.6 11.0 %all-to-all-done.1 = bf16[64,2,128]{2,1,0:T(2,128)(2,1)S(1)} async-done(((bf16[64,2,128]{2,1,0:T(2,128)(2,1)}), bf16[64,2,128]{2,1,0:T(2,128)(2,1)S(1)}, u32[]{:S(2)}, u32[]{:S(2)}) %all-to-all-start.1) | async-done | bytes 32800 | tf_op jit(solution)/shard_map/all_to_all | solution.py:134
  97.5 4.6 all-to-all-start.2
  102.1 13.5 %all-to-all-done.2 = bf16[64,2,128]{2,1,0:T(2,128)(2,1)S(1)} async-done(((bf16[64,2,128]{2,1,0:T(2,128)(2,1)}), bf16[64,2,128]{2,1,0:T(2,128)(2,1)S(1)}, u32[]{:S(2)}, u32[]{:S(2)}) %all-to-all-start.2) | async-done | bytes 32800 | tf_op jit(solution)/shard_map/all_to_all | solution.py:149
  117.3 18.8 %all-gather = bf16[16,64,128]{2,1,0:T(8,128)(2,1)S(1)} all-gather(bf16[2,64,128]{2,1,0:T(8,128)(2,1)S(1)} %bitcast.334), channel_id=2, replica_groups=mesh['region'=64,'member'=8] {'member'}, dimensions={0}, use_global_device_ids=true | all-gather | bytes 294912 | tf_op jit(solution)/shard_map/all_gather | solution.py:163
  142.6 3.6 collective-permute-done.2
  147.8 4.0 collective-permute-start.4
  154.6 23.2 %psum.51 = bf16[64,256]{0,1:T(8,128)(2,1)S(1)} all-reduce(bf16[64,256]{0,1:T(8,128)(2,1)S(1)} %bitcast.328), channel_id=1, replica_groups=mesh['region'=64,'member'=8] {'member'}, use_global_device_ids=true, to_apply=%region_11.15 | all-reduce | flops 16384 | bytes 65536 | tf_op jit(solution)/shard_map/psum | solution.py:129
  178.9 27.8 %all_to_all.69 = bf16[64,2,128]{2,1,0:T(2,128)(2,1)S(1)} all-to-all(bf16[64,2,128]{2,1,0:T(2,128)(2,1)S(1)} %reshape.612), channel_id=1, replica_groups=mesh['region'=64,'member'=8] {'region'}, dimensions={0} | all-to-all | bytes 65536 | tf_op jit(solution)/shard_map/all_to_all | solution.py:134
  209.0 17.4 %all_to_all.70 = bf16[64,2,128]{2,1,0:T(2,128)(2,1)S(1)} all-to-all(bf16[64,2,128]{2,1,0:T(2,128)(2,1)S(1)} %reshape.614), channel_id=1, replica_groups=mesh['region'=64,'member'=8] {'region'}, dimensions={0} | all-to-all | bytes 65536 | tf_op jit(solution)/shard_map/all_to_all | solution.py:149
  228.1 18.5 %all-gather.1 = bf16[16,64,128]{2,1,0:T(8,128)(2,1)S(1)} all-gather(bf16[2,64,128]{2,1,0:T(8,128)(2,1)S(1)} %bitcast.335), channel_id=3, replica_groups=mesh['region'=64,'member'=8] {'member'}, dimensions={0}, use_global_device_ids=true | all-gather | bytes 294912 | tf_op jit(solution)/shard_map/all_gather | solution.py:163
  257.6 102.0 %all-reduce.7 = (f32[]{:T(128)}, f32[]{:T(128)}) all-reduce(f32[]{:T(128)} %get-tuple-element.8, f32[]{:T(128)} %get-tuple-element.6), channel_id=1, replica_groups=mesh['region'=64,'member'=8] {'region','member'}, use_global_device_ids=true, to_apply=%region_9.13 | all-reduce | flops 2 | bytes 16 | tf_op jit(solution)/shard_map/psum | solution.py:74
  361.6 99.9 %psum.53 = f32[]{:T(128)} all-reduce(f32[]{:T(128)} %multiply_reduce_fusion), channel_id=1, replica_groups=mesh['region'=64,'member'=8] {'region','member'}, use_global_device_ids=true, to_apply=%region_18.22 | all-reduce | flops 1 | bytes 8 | tf_op jit(solution)/shard_map/psum | solution.py:74
  464.1 4.0 collective-permute-start.8
  471.2 22.7 %psum.54 = bf16[64,256]{0,1:T(8,128)(2,1)S(1)} all-reduce(bf16[64,256]{0,1:T(8,128)(2,1)S(1)} %bitcast.332), channel_id=1, replica_groups=mesh['region'=64,'member'=8] {'member'}, use_global_device_ids=true, to_apply=%region_20.24 | all-reduce | flops 16384 | bytes 65536 | tf_op jit(solution)/shard_map/psum | solution.py:129
  495.0 26.8 %all_to_all.71 = bf16[64,2,128]{2,1,0:T(2,128)(2,1)S(1)} all-to-all(bf16[64,2,128]{2,1,0:T(2,128)(2,1)S(1)} %reshape.616), channel_id=1, replica_groups=mesh['region'=64,'member'=8] {'region'}, dimensions={0} | all-to-all | bytes 65536 | tf_op jit(solution)/shard_map/all_to_all | solution.py:134
  524.1 17.4 %all_to_all.72 = bf16[64,2,128]{2,1,0:T(2,128)(2,1)S(1)} all-to-all(bf16[64,2,128]{2,1,0:T(2,128)(2,1)S(1)} %reshape.618), channel_id=1, replica_groups=mesh['region'=64,'member'=8] {'region'}, dimensions={0} | all-to-all | bytes 65536 | tf_op jit(solution)/shard_map/all_to_all | solution.py:149
  543.1 18.5 %all-gather.2 = bf16[16,64,128]{2,1,0:T(8,128)(2,1)S(1)} all-gather(bf16[2,64,128]{2,1,0:T(8,128)(2,1)S(1)} %bitcast.336), channel_id=4, replica_groups=mesh['region'=64,'member'=8] {'member'}, dimensions={0}, use_global_device_ids=true | all-gather | bytes 294912 | tf_op jit(solution)/shard_map/all_gather | solution.py:163
  568.2 3.6 collective-permute-done.10
  572.8 101.8 %psum.55 = f32[]{:T(128)} all-reduce(f32[]{:T(128)} %fusion.28), channel_id=1, replica_groups=mesh['region'=64,'member'=8] {'region','member'}, use_global_device_ids=true, to_apply=%region_25.29 | all-reduce | flops 1 | bytes 8 | tf_op jit(solution)/shard_map/psum | solution.py:179
  (161 shorter events, 70.2 us)
Async XLA Ops:
  0.0 95.3 %copy-start = (f32[8,128,128]{2,1,0:T(8,128)S(1)}, f32[8,128,128]{2,1,0:T(8,128)}, u32[]{:S(2)}) copy-start(f32[8,128,128]{2,1,0:T(8,128)} %param.25) | copy-start | bytes 1572868
  1.1 45.4 %collective-permute-start.1 = (bf16[10,64,128]{2,1,0:T(8,128)(2,1)S(1)}, bf16[10,64,128]{2,1,0:T(8,128)(2,1)S(1)}, u32[]{:S(2)}, u32[]{:S(2)}) collective-permute-start(bf16[10,64,128]{2,1,0:T(8,128)(2,1)S(1)} %convert_element_type.240), channel_id=1, source_target_pairs={{8,0},{16,8},{24,16},{32,24},{40,32},{48,40},{56,48},{64,56},{72,6... | collective-permute-start | bytes 491528 | tf_op jit(solution)/shard_map/ppermute | solution.py:22
  2.4 44.3 %collective-permute-start = (bf16[10,64,128]{2,1,0:T(8,128)(2,1)S(1)}, bf16[10,64,128]{2,1,0:T(8,128)(2,1)S(1)}, u32[]{:S(2)}, u32[]{:S(2)}) collective-permute-start(bf16[10,64,128]{2,1,0:T(8,128)(2,1)S(1)} %convert_element_type.240), channel_id=1, source_target_pairs={{0,8},{8,16},{16,24},{24,32},{32,40},{40,48},{48,56},{56,64},{64,7... | collective-permute-start | bytes 491528 | tf_op jit(solution)/shard_map/ppermute | solution.py:19
  7.0 0.7 copy-start.5
  7.0 0.7 copy-start.4
  9.9 25.2 %copy-start.7 = (bf16[4,128,128]{2,1,0:T(8,128)(2,1)S(1)}, bf16[4,128,128]{2,1,0:T(8,128)(2,1)}, u32[]{:S(2)}) copy-start(bf16[4,128,128]{2,1,0:T(8,128)(2,1)} %param.19) | copy-start | bytes 393220
  12.6 33.7 %all-to-all-start = ((s32[64,4,1]{1,2,0:T(1,128)}), s32[64,4,1]{1,2,0:T(1,128)S(1)}, u32[]{:S(2)}, u32[]{:S(2)}) async-start(s32[64,4,1]{1,2,0:T(1,128)} %bitcast.8), calls=%async_computation | async-start | bytes 65536 | tf_op jit(solution)/shard_map/all_to_all | solution.py:117
  33.6 0.7 copy-start.6
  46.5 0.7 copy-start.3
  47.2 1.0 copy-start.1
  73.7 20.9 %all-to-all-start.1 = ((bf16[64,2,128]{2,1,0:T(2,128)(2,1)}), bf16[64,2,128]{2,1,0:T(2,128)(2,1)S(1)}, u32[]{:S(2)}, u32[]{:S(2)}) async-start(bf16[64,2,128]{2,1,0:T(2,128)(2,1)} %reshape.608), calls=%async_computation.1 | async-start | bytes 65536 | tf_op jit(solution)/shard_map/all_to_all | solution.py:134
  97.5 18.1 %all-to-all-start.2 = ((bf16[64,2,128]{2,1,0:T(2,128)(2,1)}), bf16[64,2,128]{2,1,0:T(2,128)(2,1)S(1)}, u32[]{:S(2)}, u32[]{:S(2)}) async-start(bf16[64,2,128]{2,1,0:T(2,128)(2,1)} %reshape.610), calls=%async_computation.2 | async-start | bytes 65536 | tf_op jit(solution)/shard_map/all_to_all | solution.py:149
  136.5 6.0 collective-permute-start.3
  139.0 7.2 %collective-permute-start.2 = (bf16[10,64,128]{2,1,0:T(8,128)(2,1)S(1)}, bf16[10,64,128]{2,1,0:T(8,128)(2,1)S(1)}, u32[]{:S(2)}, u32[]{:S(2)}) collective-permute-start(bf16[10,64,128]{2,1,0:T(8,128)(2,1)S(1)} %fusion.19), channel_id=1, source_target_pairs={{8,0},{16,8},{24,16},{32,24},{40,32},{48,40},{56,48},{64,56},{72,6... | collective-permute-start | bytes 491528 | tf_op jit(solution)/shard_map/ppermute | solution.py:22
  140.5 5.7 copy-start.2
  146.5 6.1 collective-permute-start.5
  147.8 6.2 collective-permute-start.4
  246.9 5.9 collective-permute-start.7
  249.4 7.2 %collective-permute-start.6 = (bf16[10,64,128]{2,1,0:T(8,128)(2,1)S(1)}, bf16[10,64,128]{2,1,0:T(8,128)(2,1)S(1)}, u32[]{:S(2)}, u32[]{:S(2)}) collective-permute-start(bf16[10,64,128]{2,1,0:T(8,128)(2,1)S(1)} %fusion.20), channel_id=1, source_target_pairs={{8,0},{16,8},{24,16},{32,24},{40,32},{48,40},{56,48},{64,56},{72,6... | collective-permute-start | bytes 491528 | tf_op jit(solution)/shard_map/ppermute | solution.py:22
  462.8 7.0 %collective-permute-start.9 = (bf16[10,64,128]{2,1,0:T(8,128)(2,1)S(1)}, bf16[10,64,128]{2,1,0:T(8,128)(2,1)S(1)}, u32[]{:S(2)}, u32[]{:S(2)}) collective-permute-start(bf16[10,64,128]{2,1,0:T(8,128)(2,1)S(1)} %fusion.140), channel_id=1, source_target_pairs={{8,0},{16,8},{24,16},{32,24},{40,32},{48,40},{56,48},{64,56},{72,6... | collective-permute-start | bytes 491528 | tf_op jit(solution)/shard_map/ppermute | solution.py:22
  464.1 6.5 collective-permute-start.8
  562.0 6.0 collective-permute-start.11
  564.6 7.2 %collective-permute-start.10 = (bf16[10,64,128]{2,1,0:T(8,128)(2,1)S(1)}, bf16[10,64,128]{2,1,0:T(8,128)(2,1)S(1)}, u32[]{:S(2)}, u32[]{:S(2)}) collective-permute-start(bf16[10,64,128]{2,1,0:T(8,128)(2,1)S(1)} %fusion.21), channel_id=1, source_target_pairs={{8,0},{16,8},{24,16},{32,24},{40,32},{48,40},{56,48},{64,56},{72,6... | collective-permute-start | bytes 491528 | tf_op jit(solution)/shard_map/ppermute | solution.py:22
